TPU v7x, 32 devices: a whole 2x2x4 slice. The times are simulated.
32 devices in a mesh: layer: 2 (over y), dp: 4 (over z), feat: 4 (over x, core).
Axes of the slice: x: 2, y: 2, z: 4, core: 2. Of those that a mesh axis runs over, the one named last changes fastest.
Arguments:
- train_rows: bfloat16 [2048, 4096], P(('layer', 'dp'), 'feat'), parts along dimension 0, may hold values from -6 to 6
- train_labels: int32 [2048, 1], P(('layer', 'dp')), parts along dimension 0, may hold values from 0 to 255
- held_rows: bfloat16 [4096, 4096], P(('layer', 'dp'), 'feat'), parts along dimension 0, may hold values from -6 to 6
- held_labels: int32 [4096], P(('layer', 'dp')), parts along dimension 0, may hold values from 0 to 255
- precision: bfloat16 [6, 4096, 256], P('layer', 'feat'), parts along dimension 0
Outputs:
- pooled_cov: float32 [8192, 4096], P(('layer', 'feat'), 'dp'), parts along dimension 0
- whitened: bfloat16 [4096, 4096], P(('layer', 'dp'), 'feat'), parts along dimension 0
- distance: float32 [4096], P(('layer', 'dp')), parts along dimension 0
There are 2 independent parts, one for each index of `layer`. A program takes and returns all parts, laid end to end along the dimension named above; each array names one. Nothing has to cross between parts.
Inputs may be any that keep to these rules, and one draw needn't show every extreme that they name: `train_labels`: every class has at least one training row.
All inputs are finite; a program needn't handle non-finite values.
Results may differ from a plain program's by a relative error of at most 0.0004.
Values may be sent and summed in bfloat16 or wider, within the bound.
A program may use at most 128 MiB of HBM per device.

v0:
```python
import jax
import jax.numpy as jnp
from jax import lax
from jax.sharding import PartitionSpec as P

C = 256
BLK = 256


def padded(cells, sides, width):
    for axis, dim in sides:
        count = lax.axis_size(axis)
        ends = count - 1
        head = lax.slice_in_dim(cells, 0, width, axis=dim)
        tail = lax.slice_in_dim(cells, cells.shape[dim] - width, cells.shape[dim], axis=dim)
        cells = jnp.concatenate(
            [
                lax.ppermute(tail, axis, [(i, (i + 1) % count) for i in range(ends)]),
                cells,
                lax.ppermute(head, axis, [((i + 1) % count, i) for i in range(ends)]),
            ],
            axis=dim,
        )
    return cells


def contract_rows(left, right):
    return lax.dot_general(
        left, right, (((0,), (0,)), ((), ())), preferred_element_type=jnp.float32
    )


def body(train_rows, train_labels, held_rows, held_labels, precision):
    local = train_rows.shape[1]
    full = lax.all_gather(train_rows, "feat", axis=1, tiled=True)
    width = full.shape[1]
    classes = jnp.arange(C, dtype=jnp.int32)
    onehot_train = (train_labels == classes[None, :]).astype(jnp.bfloat16)
    local_sums = contract_rows(onehot_train, full)
    local_counts = jnp.sum(onehot_train.astype(jnp.float32), axis=0)
    sums, counts = lax.psum((local_sums, local_counts), "dp")
    means = sums / counts[:, None]
    feat_index = lax.axis_index("feat")
    dp_index = lax.axis_index("dp")
    dp_count = lax.axis_size("dp")
    ncols = width // dp_count
    block = lax.psum_scatter(
        contract_rows(full, train_rows), "dp", scatter_dimension=0, tiled=True
    ).T
    sums_rows = lax.dynamic_slice_in_dim(sums, feat_index * local, local, 1)
    means_cols = lax.dynamic_slice_in_dim(means, dp_index * ncols, ncols, 1)
    correction = lax.dot_general(
        sums_rows,
        means_cols,
        (((0,), (0,)), ((), ())),
        precision=lax.Precision.HIGHEST,
        preferred_element_type=jnp.float32,
    )
    denominator = float(train_rows.shape[0] * dp_count - C)
    pooled_cov = (block - correction) / denominator
    means_local = lax.dynamic_slice_in_dim(means, feat_index * local, local, 1)
    picked = means_local[held_labels]
    centred = held_rows.astype(jnp.float32) - picked
    extended = padded(centred, (("feat", 1),), BLK)
    held_count = held_rows.shape[0]
    nlocal = local // BLK
    windows = extended.reshape(held_count, nlocal + 2, BLK)
    bands = precision.astype(jnp.float32).reshape(3, nlocal, BLK, BLK)
    image = jnp.zeros((held_count, nlocal, BLK), jnp.float32)
    for k in range(3):
        image = image + jnp.einsum(
            "rmj,mij->rmi",
            windows[:, k : k + nlocal],
            bands[k],
            precision=lax.Precision.HIGHEST,
            preferred_element_type=jnp.float32,
        )
    image = image.reshape(held_count, local)
    partial_score = jnp.sum(centred * image, axis=1)
    distance = lax.psum(partial_score, "feat") / width
    return (pooled_cov, image.astype(jnp.bfloat16), distance)


def solution(mesh):
    return jax.shard_map(
        body,
        mesh=mesh,
        in_specs=(
            P(("layer", "dp"), "feat"),
            P(("layer", "dp"), None),
            P(("layer", "dp"), "feat"),
            P(("layer", "dp")),
            P("layer", "feat", None),
        ),
        out_specs=(P(("layer", "feat"), "dp"), P(("layer", "dp"), "feat"), P(("layer", "dp"))),
        check_vma=False,
    )
```

profile of v0, /device:TPU:0, one launch (start us, length us, event | category | flops | bytes accessed | tf_op | source)
XLA Modules:
  0.0 497.0 jit_solution(6147197103815917250)
XLA Ops:
  7.9 26.9 %all-gather.2.cloned.1.call-done = bf16[256,4096]{1,0:T(8,128)(2,1)} async-done(((bf16[256,1024]{1,0:T(8,128)(2,1)}), bf16[256,4096]{1,0:T(8,128)(2,1)}) %all-gather.2.cloned.1.call-update) | async-done | bytes 2097168 | tf_op jit(solution)/shard_map/all_gather | solution.py:35
  34.9 4.4 fusion.4
  39.4 1.5 copy-done.3
  41.0 8.7 %fusion.9 = f32[4096,1024]{1,0:T(8,128)} fusion(bf16[256,4096]{1,0:T(8,128)(2,1)S(1)} %copy-done.3, bf16[256,1024]{1,0:T(8,128)(2,1)S(1)} %copy-done.4), kind=kOutput, calls=%fused_computation.22 | convolution fusion | flops 2147483648 | bytes 19398656 | tf_op jit(solution)/shard_map/dot_general | solution.py:28
  50.5 12.1 %psum.22 = f32[256]{0:T(256)S(1)} all-reduce(f32[256]{0:T(256)S(1)} %convert_reduce_fusion), channel_id=1, replica_groups=mesh['layer'=2,'dp'=4,'feat'=4] {'dp'}, use_global_device_ids=true, to_apply=%region_3.0 | all-reduce | flops 256 | bytes 2048 | tf_op jit(solution)/shard_map/psum | solution.py:41
  62.6 132.1 %all-reduce.2.cloned.1.call-done = f32[256,4096]{1,0:T(8,128)} async-done(((f32[256,4096]{1,0:T(8,128)}), f32[256,4096]{1,0:T(8,128)}) %all-reduce.2.cloned.1.call-update) | async-done | bytes 4194320 | tf_op jit(solution)/shard_map/psum | solution.py:41
  194.7 2.7 broadcast_divide_fusion
  197.4 2.0 copy-done.2
  199.5 2.6 gather_fusion
  202.2 2.2 convert_subtract_fusion
  204.3 1.2 fusion.7
  205.6 1.3 collective-permute-start.1
  206.9 3.1 collective-permute-start
  209.9 2.5 fusion.8
  212.5 2.0 pad_maximum_fusion
  214.5 2.4 copy.21
  216.9 2.3 fusion.10
  220.4 2.6 add_add_fusion
  223.0 3.1 copy.25
  226.1 3.5 multiply_reduce_fusion
  229.6 11.3 %psum.23 = f32[512]{0:T(512)S(1)} all-reduce(f32[512]{0:T(512)S(1)} %get-tuple-element.12), channel_id=1, replica_groups=mesh['layer'=2,'dp'=4,'feat'=4] {'feat'}, use_global_device_ids=true, to_apply=%region_5.0 | all-reduce | flops 512 | bytes 4096 | tf_op jit(solution)/shard_map/psum | solution.py:80
  241.6 235.0 %reduce-scatter.2.cloned.1.call-done = f32[1024,1024]{1,0:T(8,128)} async-done(((f32[4096,1024]{1,0:T(8,128)}), f32[1024,1024]{1,0:T(8,128)}) %reduce-scatter.2.cloned.1.call-update) | async-done | bytes 4194320 | tf_op jit(solution)/shard_map/reduce_scatter | solution.py:47
  476.5 8.6 %fusion = f32[1024,1024]{0,1:T(8,128)} fusion(f32[1024,1024]{1,0:T(8,128)} %reduce-scatter.2.cloned.1.call-done, f32[256,4096]{1,0:T(8,128)} %copy-done.2, s32[]{:T(128)S(6)} %select_n.11, f32[256,4096]{1,0:T(8,128)} %all-reduce.2.cloned.1.call-done, s32[]{:T(128)S(6)} %select_n.10), kind=kOutput, calls=%fused_computation.2 | convolution fusion | flops 3223322624 | bytes 10485768 | tf_op jit(solution)/shard_map/dot_general | solution.py:52
  485.1 5.3 %copy.27 = f32[1024,1024]{1,0:T(8,128)} copy(f32[1024,1024]{0,1:T(8,128)} %fusion) | data formatting | bytes 8388608
  (32 shorter events, 3.6 us)
Async XLA Ops:
  7.2 27.7 %all-gather.2.cloned.1.call-start = ((), (), s32[]{:S(2)}) async-start(), calls=%async_computation.1 | async-start | bytes 2621440 | tf_op jit(solution)/shard_map/all_gather | solution.py:35
  7.9 186.8 %all-reduce.2.cloned.1.call-start = ((), (), s32[]{:S(2)}) async-start(), calls=%async_computation.3 | async-start | bytes 8388608 | tf_op jit(solution)/shard_map/psum | solution.py:41
  39.3 1.6 copy-start.3
  39.3 1.7 copy-start.4
  39.4 437.2 %reduce-scatter.2.cloned.1.call-start = ((), (), s32[]{:S(2)}) async-start(), calls=%async_computation.2 | async-start | bytes 20971520 | tf_op jit(solution)/shard_map/reduce_scatter | solution.py:47
  49.7 0.7 copy-start.8
  49.7 12.8 %copy-start.9 = (s32[512]{0:T(512)S(1)}, s32[512]{0:T(512)}, u32[]{:S(2)}) copy-start(s32[512]{0:T(512)} %param.8) | copy-start | bytes 6148
  197.4 2.0 copy-start.2
  199.5 2.7 copy-start.7
  204.3 8.2 %copy-start = (f32[512,1024]{1,0:T(8,128)}, f32[512,1024]{1,0:T(8,128)S(1)}, u32[]{:S(2)}) copy-start(f32[512,1024]{1,0:T(8,128)S(1)} %convert_subtract_fusion) | copy-start | bytes 6291460
  205.6 6.9 %collective-permute-start.1 = (f32[512,256]{1,0:T(8,128)}, f32[512,256]{1,0:T(8,128)S(1)}, u32[]{:S(2)}, u32[]{:S(2)}) collective-permute-start(f32[512,256]{1,0:T(8,128)} %get-tuple-element.15), channel_id=1, source_target_pairs={{1,0},{2,1},{3,2},{5,4},{6,5},{7,6},{9,8},{10,9},{11,10},{13,12},{... | collective-permute-start | bytes 1572872 | tf_op jit(solution)/shard_map/ppermute | solution.py:20
  206.9 5.6 %collective-permute-start = (f32[512,256]{1,0:T(8,128)}, f32[512,256]{1,0:T(8,128)S(1)}, u32[]{:S(2)}, u32[]{:S(2)}) collective-permute-start(f32[512,256]{1,0:T(8,128)} %get-tuple-element.14), channel_id=1, source_target_pairs={{0,1},{1,2},{2,3},{4,5},{5,6},{6,7},{8,9},{9,10},{10,11},{12,13},{... | collective-permute-start | bytes 1572872 | tf_op jit(solution)/shard_map/ppermute | solution.py:18
  216.9 2.3 copy-start.6
  219.2 1.2 copy-start.5
  223.0 3.1 copy-start.1
Sparse Core Ops, SparseCore 0:
  9.6 25.2 all-gather.1
  39.5 155.1 all-reduce.1
  197.2 279.3 reduce-scatter.1
where the time goes:
time: 497 us
  waiting for transfers between devices  395 us (79%)
  matrix products  27.8 us (6%)
  blocking collectives  23.4 us (5%)
  local copies, waits for them, and re-layouts  21.6 us (4%)
  between operations  13.9 us (3%)
  other arithmetic  11.1 us (2%)
    reduce_scatter x1, waiting for transfers between devices, body(): lax.psum_scatter(contract_rows(full, train_rows), 'dp', scatter_dimension...  235 us
    psum x1, waiting for transfers between devices, body(): sums, counts = lax.psum((local_sums, local_counts), 'dp')  132 us
    all_gather x1, waiting for transfers between devices, body(): full = lax.all_gather(train_rows, 'feat', axis=1, tiled=True)  26.9 us
    dot_general x2, matrix products, contract_rows(): lax.dot_general(left, right, (((0,), (0,)), ((), ())), preferred_element_...  13.2 us
    psum x1, blocking collectives, body(): sums, counts = lax.psum((local_sums, local_counts), 'dp')  12.1 us
    psum x1, blocking collectives, body(): distance = lax.psum(partial_score, 'feat') / width  11.3 us
  transfers between devices with their start and end apart: 5, of which 3 were waited for; matrix products, arithmetic and copies ran while one was open for 8% of the time, Pallas kernels for 0%

commit v1 on v0

--- a/solution.py
+++ b/solution.py
@@ -1,10 +1,16 @@
 import jax
 import jax.numpy as jnp
 from jax import lax
+from jax.experimental import pallas as pl
+from jax.experimental.pallas import tpu as pltpu
 from jax.sharding import PartitionSpec as P
 
 C = 256
 BLK = 256
+MESH = pl.DeviceIdType.MESH
+F32 = jnp.float32
+BF16 = jnp.bfloat16
+CHUNKS = 4
 
 
 def padded(cells, sides, width):
@@ -30,7 +36,7 @@
     )
 
 
-def body(train_rows, train_labels, held_rows, held_labels, precision):
+def general_body(train_rows, train_labels, held_rows, held_labels, precision):
     local = train_rows.shape[1]
     full = lax.all_gather(train_rows, "feat", axis=1, tiled=True)
     width = full.shape[1]
@@ -81,9 +87,421 @@
     return (pooled_cov, image.astype(jnp.bfloat16), distance)
 
 
+def nt(left, right):
+    return lax.dot_general(left, right, (((1,), (1,)), ((), ())), preferred_element_type=F32)
+
+
+def nn(left, right):
+    return lax.dot_general(left, right, (((1,), (0,)), ((), ())), preferred_element_type=F32)
+
+
+def split(value):
+    high = value.astype(BF16)
+    return high, (value - high.astype(F32)).astype(BF16)
+
+
+def gather_kernel(
+    train, labels, held, held_labels, prec,
+    lhs, rhs, white, dist,
+    tf, td, tail_l, tail_r, lab, hext, mhi, mlo, img, onehot_t, onehot_h, dacc, dsend, drecv,
+    z_recv, up_send, dn_send, d_recv, sib_send, och_send,
+    lab_send, lab_recv, he_send, he_recv, me_send, me_recv, ds_send, ds_recv, own_sem, out_sem,
+):
+    n = 4
+    f = lax.axis_index("feat")
+    z = lax.axis_index("dp")
+    rows, local = train.shape
+    nheld = held.shape[0]
+    nloc = local // BLK
+    cr = rows // CHUNKS
+    core = lax.rem(f, 2)
+    sib = f + 1 - 2 * core
+    chip = f // 2
+    ochip = 1 - chip
+    root = f == z
+    near = chip == z // 2
+
+    def others(i):
+        return [lax.rem(i + s, n) for s in range(1, n)]
+
+    barrier = pltpu.get_barrier_semaphore()
+    for o in others(z):
+        pl.semaphore_signal(barrier, inc=1, device_id={"dp": o}, device_id_type=MESH)
+    for o in others(f):
+        pl.semaphore_signal(barrier, inc=1, device_id={"feat": o}, device_id_type=MESH)
+    pl.semaphore_wait(barrier, 2 * (n - 1))
+
+    def remote(src, dst, send, recv, where):
+        return pltpu.make_async_remote_copy(
+            src_ref=src, dst_ref=dst, send_sem=send, recv_sem=recv,
+            device_id=where, device_id_type=MESH,
+        )
+
+    def part(c):
+        return pl.ds(pl.multiple_of(c * cr, cr), cr)
+
+    up = {"dp": jnp.minimum(z + 1, n - 1)}
+    dn = {"dp": jnp.maximum(z - 1, 0)}
+
+    def up_copy(o, c, src):
+        return remote(src, tf.at[o, part(c)], up_send.at[o, c], z_recv.at[o, c], up)
+
+    def dn_copy(o, c, src):
+        return remote(src, tf.at[o, part(c)], dn_send.at[o, c], z_recv.at[o, c], dn)
+
+    def sib_copy(o, c, src):
+        return remote(src, td.at[o, part(c)], sib_send.at[o, c], d_recv.at[o, c], {"feat": sib})
+
+    def och_copy(o, c, src):
+        where = {"feat": 2 * ochip + lax.rem(c, 2)}
+        return remote(src, td.at[o, part(c)], och_send.at[o, c], d_recv.at[o, c], where)
+
+    def own_copy(o, c, src):
+        return pltpu.make_async_copy(src, td.at[o, part(c)], own_sem.at[o, c])
+
+    def send_on(o, c, src):
+        @pl.when((o <= z) & (z < n - 1))
+        def _():
+            up_copy(o, c, src).start()
+
+        @pl.when((o >= z) & (z > 0))
+        def _():
+            dn_copy(o, c, src).start()
+
+        @pl.when(root)
+        def _():
+            och_copy(o, c, src).start()
+            sib_copy(o, c, src).start()
+            own_copy(o, c, src).start()
+
+    def tf_event(o, c):
+        src = tf.at[o, part(c)]
+        up_copy(o, c, src).wait_recv()
+        send_on(o, c, src)
+
+    def td_event(o, c):
+        dst = td.at[o, part(c)]
+
+        @pl.when(root)
+        def _():
+            own_copy(o, c, tf.at[o, part(c)]).wait()
+
+        @pl.when(jnp.logical_not(root))
+        def _():
+            sib_copy(o, c, dst).wait_recv()
+
+        @pl.when(jnp.logical_not(near) & (lax.rem(c, 2) == core))
+        def _():
+            sib_copy(o, c, dst).start()
+
+    lab_copies = [
+        remote(labels, lab.at[z], lab_send.at[i], lab_recv.at[z], {"dp": o})
+        for i, o in enumerate(others(z))
+    ]
+    for copy in lab_copies:
+        copy.start()
+
+    @pl.loop(0, CHUNKS)
+    def _(c):
+        send_on(z, c, train.at[part(c)])
+
+    left = {"feat": jnp.maximum(f - 1, 0)}
+    right = {"feat": jnp.minimum(f + 1, n - 1)}
+    first = pl.ds(0, BLK)
+    last = pl.ds(local + BLK, BLK)
+    head = pl.ds(BLK, BLK)
+    end = pl.ds(local, BLK)
+
+    he_left = remote(
+        held.at[:, pl.ds(0, BLK)], hext.at[:, last], he_send.at[0], he_recv.at[1], left
+    )
+    he_right = remote(
+        held.at[:, pl.ds(local - BLK, BLK)], hext.at[:, first], he_send.at[1], he_recv.at[0], right
+    )
+
+    @pl.when(f > 0)
+    def _():
+        he_left.start()
+
+    @pl.when(f < n - 1)
+    def _():
+        he_right.start()
+
+    tf[z] = train[...]
+    lab[z] = labels[...]
+    hext[:, pl.ds(BLK, local)] = held[...]
+
+    @pl.when(f == 0)
+    def _():
+        hext[:, first] = jnp.zeros((nheld, BLK), BF16)
+        mhi[:, first] = jnp.zeros((C, BLK), BF16)
+        mlo[:, first] = jnp.zeros((C, BLK), BF16)
+
+    @pl.when(f == n - 1)
+    def _():
+        hext[:, last] = jnp.zeros((nheld, BLK), BF16)
+        mhi[:, last] = jnp.zeros((C, BLK), BF16)
+        mlo[:, last] = jnp.zeros((C, BLK), BF16)
+
+    classes = lax.broadcasted_iota(jnp.int32, (C, nheld), 0)
+    hot = (held_labels[0:1, :] == classes).astype(F32)
+    onehot_h[...] = hot.T.astype(BF16)
+
+    @pl.when(f > 0)
+    def _():
+        he_right.wait_recv()
+
+    @pl.when(f < n - 1)
+    def _():
+        he_left.wait_recv()
+
+    def block(i):
+        return pl.ds(pl.multiple_of(i * BLK, BLK), BLK)
+
+    @pl.loop(0, nloc)
+    def _(m):
+        total = nt(hext[:, block(m)], prec[0, block(m), :])
+        for k in (1, 2):
+            total += nt(hext[:, block(m + k)], prec[k, block(m), :])
+        img[:, block(m)] = total
+
+    for i, o in enumerate(others(z)):
+        remote(labels, lab.at[o], lab_send.at[i], lab_recv.at[o], {"dp": o}).wait_recv()
+    for o in range(n):
+        ids = lax.broadcasted_iota(jnp.int32, (C, rows), 0)
+        onehot_t[:, o * rows : (o + 1) * rows] = (lab[o, 0:1, :] == ids).astype(F32).astype(BF16)
+
+    def out_copies(o):
+        where = pl.ds(pl.multiple_of(o * rows, rows), rows)
+        return (
+            pltpu.make_async_copy(tf.at[o], lhs.at[where], out_sem.at[0, o]),
+            pltpu.make_async_copy(td.at[o], rhs.at[where], out_sem.at[1, o]),
+        )
+
+    @pl.loop(0, CHUNKS)
+    def _(c):
+        td_event(z, c)
+
+    for s in range(1, n):
+
+        @pl.loop(0, CHUNKS + 1)
+        def _(c, s=s):
+            for o in (z - s, z + s):
+
+                @pl.when((o >= 0) & (o < n) & (c < CHUNKS))
+                def _():
+                    tf_event(o, c)
+
+            for o in (z - s, z + s):
+
+                @pl.when((o >= 0) & (o < n) & (c > 0))
+                def _():
+                    td_event(o, c - 1)
+
+    for o in range(n):
+        for copy in out_copies(o):
+            copy.start()
+
+    counts = jnp.sum(onehot_t[...].astype(F32), axis=1, keepdims=True)
+    inverse = 1.0 / counts
+
+    @pl.loop(0, nloc)
+    def _(m):
+        total = nn(onehot_t[:, 0:rows], tf[0, :, block(m)])
+        for o in range(1, n):
+            total += nn(onehot_t[:, o * rows : (o + 1) * rows], tf[o, :, block(m)])
+        high, low = split(total)
+        tail_l[0:C, block(m)] = high
+        tail_l[C : 2 * C, block(m)] = high
+        tail_l[2 * C : 3 * C, block(m)] = low
+        high, low = split(total * inverse)
+        mhi[:, block(m + 1)] = high
+        mlo[:, block(m + 1)] = low
+
+    me_left = [
+        remote(ref.at[:, head], ref.at[:, last], me_send.at[0, i], me_recv.at[1, i], left)
+        for i, ref in enumerate((mhi, mlo))
+    ]
+    me_right = [
+        remote(ref.at[:, end], ref.at[:, first], me_send.at[1, i], me_recv.at[0, i], right)
+        for i, ref in enumerate((mhi, mlo))
+    ]
+
+    @pl.when(f > 0)
+    def _():
+        for copy in me_left:
+            copy.start()
+
+    @pl.when(f < n - 1)
+    def _():
+        for copy in me_right:
+            copy.start()
+
+    @pl.loop(0, nloc)
+    def _(m):
+        total = nn(onehot_t[:, 0:rows], td[0, :, block(m)])
+        for o in range(1, n):
+            total += nn(onehot_t[:, o * rows : (o + 1) * rows], td[o, :, block(m)])
+        high, low = split(-(total * inverse))
+        tail_r[0:C, block(m)] = high
+        tail_r[C : 2 * C, block(m)] = low
+        tail_r[2 * C : 3 * C, block(m)] = high
+
+    below = pl.ds(n * rows, 3 * C)
+    tail_copies = (
+        pltpu.make_async_copy(tail_l, lhs.at[below], out_sem.at[0, n]),
+        pltpu.make_async_copy(tail_r, rhs.at[below], out_sem.at[1, n]),
+    )
+    for copy in tail_copies:
+        copy.start()
+
+    @pl.when(f > 0)
+    def _():
+        for copy in me_right:
+            copy.wait_recv()
+
+    @pl.when(f < n - 1)
+    def _():
+        for copy in me_left:
+            copy.wait_recv()
+
+    dacc[...] = jnp.zeros_like(dacc)
+
+    @pl.loop(0, nloc)
+    def _(m):
+        shift = jnp.zeros((C, BLK), F32)
+        for k in range(3):
+            band = prec[k, block(m), :]
+            shift += nt(mhi[:, block(m + k)], band) + nt(mlo[:, block(m + k)], band)
+        high, low = split(shift)
+        pick = onehot_h[...]
+        image = img[:, block(m)] - (nn(pick, high) + nn(pick, low))
+        white[:, block(m)] = image.astype(BF16)
+        picked = nn(pick, mhi[:, block(m + 1)]) + nn(pick, mlo[:, block(m + 1)])
+        score = (held[:, block(m)].astype(F32) - picked) * image
+        dacc[...] += score[:, 0:128] + score[:, 128:256]
+
+    row = jnp.sum(dacc[...].T, axis=0, keepdims=True)
+    dsend[...] = jnp.broadcast_to(row, dsend.shape)
+    ds_copies = [
+        remote(dsend, drecv.at[f], ds_send.at[i], ds_recv.at[f], {"feat": o})
+        for i, o in enumerate(others(f))
+    ]
+    for copy in ds_copies:
+        copy.start()
+    for i, o in enumerate(others(f)):
+        remote(dsend, drecv.at[o], ds_send.at[i], ds_recv.at[o], {"feat": o}).wait_recv()
+    total = row
+    for o in others(f):
+        total += drecv[o, 0:1, :]
+    dist[...] = total * (1.0 / (local * n))
+
+    for copy in lab_copies + ds_copies:
+        copy.wait_send()
+
+    @pl.when(f > 0)
+    def _():
+        for copy in [he_left] + me_left:
+            copy.wait_send()
+
+    @pl.when(f < n - 1)
+    def _():
+        for copy in [he_right] + me_right:
+            copy.wait_send()
+
+    @pl.loop(0, n * CHUNKS)
+    def _(i):
+        o = i // CHUNKS
+        c = lax.rem(i, CHUNKS)
+        src = tf.at[o, part(c)]
+
+        @pl.when((o <= z) & (z < n - 1))
+        def _():
+            up_copy(o, c, src).wait_send()
+
+        @pl.when((o >= z) & (z > 0))
+        def _():
+            dn_copy(o, c, src).wait_send()
+
+        @pl.when(root)
+        def _():
+            och_copy(o, c, src).wait_send()
+
+        @pl.when(root | (jnp.logical_not(near) & (lax.rem(c, 2) == core)))
+        def _():
+            sib_copy(o, c, src).wait_send()
+
+    for o in range(n):
+        for copy in out_copies(o):
+            copy.wait()
+    for copy in tail_copies:
+        copy.wait()
+
+
+def square_body(train_rows, train_labels, held_rows, held_labels, precision):
+    rows, local = train_rows.shape
+    nheld = held_rows.shape[0]
+    n = lax.axis_size("dp")
+    labels = jnp.broadcast_to(train_labels.reshape(1, rows), (8, rows))
+    hlabels = jnp.broadcast_to(held_labels.reshape(1, nheld), (8, nheld))
+    depth = n * rows + 3 * C
+    vmem = pl.BlockSpec(memory_space=pltpu.VMEM)
+    hbm = pl.BlockSpec(memory_space=pl.ANY)
+    dma = pltpu.SemaphoreType.DMA
+    lhs, rhs, white, dist = pl.pallas_call(
+        gather_kernel,
+        out_shape=(
+            jax.ShapeDtypeStruct((depth, local), BF16),
+            jax.ShapeDtypeStruct((depth, local), BF16),
+            jax.ShapeDtypeStruct((nheld, local), BF16),
+            jax.ShapeDtypeStruct((1, nheld), F32),
+        ),
+        in_specs=[vmem] * 5,
+        out_specs=(hbm, hbm, vmem, vmem),
+        scratch_shapes=[
+            pltpu.VMEM((n, rows, local), BF16),
+            pltpu.VMEM((n, rows, local), BF16),
+            pltpu.VMEM((3 * C, local), BF16),
+            pltpu.VMEM((3 * C, local), BF16),
+            pltpu.VMEM((n, 8, rows), jnp.int32),
+            pltpu.VMEM((nheld, local + 2 * BLK), BF16),
+            pltpu.VMEM((C, local + 2 * BLK), BF16),
+            pltpu.VMEM((C, local + 2 * BLK), BF16),
+            pltpu.VMEM((nheld, local), F32),
+            pltpu.VMEM((C, n * rows), BF16),
+            pltpu.VMEM((nheld, C), BF16),
+            pltpu.VMEM((nheld, 128), F32),
+            pltpu.VMEM((8, nheld), F32),
+            pltpu.VMEM((n, 8, nheld), F32),
+            dma((n, CHUNKS)),
+            dma((n, CHUNKS)),
+            dma((n, CHUNKS)),
+            dma((n, CHUNKS)),
+            dma((n, CHUNKS)),
+            dma((n, CHUNKS)),
+            dma((n - 1,)),
+            dma((n,)),
+            dma((2,)),
+            dma((2,)),
+            dma((2, 2)),
+            dma((2, 2)),
+            dma((n - 1,)),
+            dma((n,)),
+            dma((n, CHUNKS)),
+            dma((2, n + 1)),
+        ],
+        compiler_params=pltpu.CompilerParams(
+            collective_id=0, has_side_effects=True, vmem_limit_bytes=40 * 1024 * 1024
+        ),
+    )(train_rows, labels, held_rows, hlabels, precision)
+    pooled_cov = contract_rows(lhs, rhs) * (1.0 / float(rows * n - C))
+    return pooled_cov, white, dist.reshape(nheld)
+
+
 def solution(mesh):
+    square = mesh.shape["dp"] == 4 and mesh.shape["feat"] == 4
     return jax.shard_map(
-        body,
+        square_body if square else general_body,
         mesh=mesh,
         in_specs=(
             P(("layer", "dp"), "feat"),

time: 497 us -> 73.7 us (0.15)
  waiting for transfers between devices: 395 us -> 0 us
  Pallas kernels: 0 us -> 60.7 us
  blocking collectives: 23.4 us -> 0 us
  matrix products: 27.8 us -> 5.55 us
  local copies, waits for them, and re-layouts: 21.6 us -> 6.58 us
  between operations: 13.9 us -> 0.64 us
  other arithmetic: 11.1 us -> 0 us
    reduce_scatter x1 -> x0, waiting for transfers between devices: 235 us -> none  [body(): lax.psum_scatter(contract_rows(full, train_rows), 'dp', scatter_dimension...]
    psum x1 -> x0, waiting for transfers between devices: 132 us -> none  [body(): sums, counts = lax.psum((local_sums, local_counts), 'dp')]
    pallas_call x0 -> x1, Pallas kernels: none -> 60.7 us  [square_body(): pl.pallas_call(gather_kernel, out_shape=(jax.ShapeDtypeStruct((depth, loc...]
    all_gather x1 -> x0, waiting for transfers between devices: 26.9 us -> none  [body(): full = lax.all_gather(train_rows, 'feat', axis=1, tiled=True)]
    psum x2 -> x0, blocking collectives: 23.4 us -> none  [the longest x1 12.1 us: body(): sums, counts = lax.psum((local_sums, local_counts), 'dp')]
    dot_general x4 -> x0, matrix products: 14.7 us -> none  [the longest x1 8.56 us: body(): lax.dot_general(sums_rows, means_cols, (((0,), (0,)), ((), ())), precisio...]
    dot_general x2 -> x1, matrix products: 13.2 us -> 5.55 us  [contract_rows(): lax.dot_general(left, right, (((0,), (0,)), ((), ())), preferred_element_...]
  transfers between devices with their start and end apart: 5 -> 0, of which waited for: 3 -> 0; matrix products, arithmetic and copies ran while one was open for 8% -> 0% of each run, Pallas kernels for 0% -> 0%
where the time goes in v1:
time: 73.7 us; the launch traced here: 73.5 us
  Pallas kernels  60.7 us (82%)
  local copies, waits for them, and re-layouts  6.58 us (9%)
  matrix products  5.55 us (8%)
    pallas_call x1, Pallas kernels, square_body(): pl.pallas_call(gather_kernel, out_shape=(jax.ShapeDtypeStruct((depth, loc...  60.7 us
    dot_general x1, matrix products, contract_rows(): lax.dot_general(left, right, (((0,), (0,)), ((), ())), preferred_element_...  5.55 us
    unnamed x8, local copies, waits for them, and re-layouts  5.22 us

profile of v1, /device:TPU:0, one launch (start us, length us, event | category | flops | bytes accessed | tf_op | source)
XLA Modules:
  0.0 73.5 jit_solution(10217679250975225210)
XLA Ops:
  0.6 0.7 broadcast_in_dim.13.labels
  1.3 0.7 broadcast_in_dim.14.held_labels
  2.0 0.0 copy-start
  2.0 1.4 %copy-done = bf16[3,1024,256]{2,1,0:T(8,128)(2,1)S(1)} copy-done((bf16[3,1024,256]{2,1,0:T(8,128)(2,1)S(1)}, bf16[3,1024,256]{2,1,0:T(8,128)(2,1)}, u32[]{:S(2)}) %copy-start) | copy-done | bytes 1572888
  3.4 0.0 copy-start.1
  3.4 1.2 %copy-done.1 = bf16[512,1024]{1,0:T(8,128)(2,1)S(1)} copy-done((bf16[512,1024]{1,0:T(8,128)(2,1)S(1)}, bf16[512,1024]{1,0:T(8,128)(2,1)}, u32[]{:S(2)}) %copy-start.1) | copy-done | bytes 1048600
  4.6 0.0 copy-start.2
  4.6 1.0 %copy-done.2 = bf16[256,1024]{1,0:T(8,128)(2,1)S(1)} copy-done((bf16[256,1024]{1,0:T(8,128)(2,1)S(1)}, bf16[256,1024]{1,0:T(8,128)(2,1)}, u32[]{:S(2)}) %copy-start.2) | copy-done | bytes 524312
  5.7 60.7 %shard_map.76 = (bf16[1792,1024]{1,0:T(8,128)(2,1)S(1)}, bf16[1792,1024]{1,0:T(8,128)(2,1)S(1)}, bf16[512,1024]{1,0:T(8,128)(2,1)S(1)}, f32[1,512]{1,0:T(1,128)S(1)}) custom-call(bf16[256,1024]{1,0:T(8,128)(2,1)S(1)} %copy-done.2, s32[8,256]{1,0:T(8,128)S(1)} %broadcast_in_dim.13.labels, bf16[512,1024]{1,0:T(8,128)(2,1)S(1)} %copy-done.1, ...), custom_call_target="tpu_custom_call" | custom-call | tf_op jit(solution)/shard_map/pallas_call | solution.py:451
  66.4 5.6 %convolution_multiply_fusion = f32[1024,1024]{1,0:T(8,128)} fusion(bf16[1792,1024]{1,0:T(8,128)(2,1)S(1)} %get-tuple-element.7, bf16[1792,1024]{1,0:T(8,128)(2,1)S(1)} %get-tuple-element.8), kind=kOutput, calls=%fused_computation | convolution fusion | flops 3759144960 | bytes 11534336 | tf_op jit(solution)/shard_map/dot_general | solution.py:34
  71.9 1.0 %copy.10 = bf16[512,1024]{1,0:T(8,128)(2,1)} copy(bf16[512,1024]{1,0:T(8,128)(2,1)S(1)} %get-tuple-element.15) | data formatting | bytes 2097152
  72.9 0.6 copy.11
Async XLA Ops:
  2.0 1.4 %copy-start = (bf16[3,1024,256]{2,1,0:T(8,128)(2,1)S(1)}, bf16[3,1024,256]{2,1,0:T(8,128)(2,1)}, u32[]{:S(2)}) copy-start(bf16[3,1024,256]{2,1,0:T(8,128)(2,1)} %prec.1) | copy-start | bytes 4718596
  3.4 1.2 %copy-start.1 = (bf16[512,1024]{1,0:T(8,128)(2,1)S(1)}, bf16[512,1024]{1,0:T(8,128)(2,1)}, u32[]{:S(2)}) copy-start(bf16[512,1024]{1,0:T(8,128)(2,1)} %held.1) | copy-start | bytes 3145732
  4.6 1.0 %copy-start.2 = (bf16[256,1024]{1,0:T(8,128)(2,1)S(1)}, bf16[256,1024]{1,0:T(8,128)(2,1)}, u32[]{:S(2)}) copy-start(bf16[256,1024]{1,0:T(8,128)(2,1)} %train.1) | copy-start | bytes 1572868

commit v2 on v1

--- a/solution.py
+++ b/solution.py
@@ -101,17 +101,18 @@
 
 
 def gather_kernel(
-    train, labels, held, held_labels, prec,
-    lhs, rhs, white, dist,
-    tf, td, tail_l, tail_r, lab, hext, mhi, mlo, img, onehot_t, onehot_h, dacc, dsend, drecv,
+    train_hbm, labels, held_hbm, held_labels, prec_hbm,
+    cov, white, dist,
+    train, prec, tf, td, sf, sd, tail_l, tail_r, lab, hext, mhi, mlo, img, onehot_t, onehot_h,
+    dacc, dsend, drecv,
     z_recv, up_send, dn_send, d_recv, sib_send, och_send,
-    lab_send, lab_recv, he_send, he_recv, me_send, me_recv, ds_send, ds_recv, own_sem, out_sem,
+    lab_send, lab_recv, he_send, he_recv, me_send, me_recv, ds_send, ds_recv, own_sem, in_sem,
 ):
     n = 4
     f = lax.axis_index("feat")
     z = lax.axis_index("dp")
     rows, local = train.shape
-    nheld = held.shape[0]
+    nheld = held_hbm.shape[0]
     nloc = local // BLK
     cr = rows // CHUNKS
     core = lax.rem(f, 2)
@@ -124,6 +125,12 @@
     def others(i):
         return [lax.rem(i + s, n) for s in range(1, n)]
 
+    train_in = pltpu.make_async_copy(train_hbm, train, in_sem.at[0])
+    held_in = pltpu.make_async_copy(held_hbm, hext.at[:, pl.ds(BLK, local)], in_sem.at[1])
+    prec_in = pltpu.make_async_copy(prec_hbm, prec, in_sem.at[2])
+    for copy in (train_in, held_in, prec_in):
+        copy.start()
+
     barrier = pltpu.get_barrier_semaphore()
     for o in others(z):
         pl.semaphore_signal(barrier, inc=1, device_id={"dp": o}, device_id_type=MESH)
@@ -194,12 +201,16 @@
         def _():
             sib_copy(o, c, dst).start()
 
+    lab[z] = jnp.broadcast_to(labels[...], lab.shape[1:])
+
     lab_copies = [
-        remote(labels, lab.at[z], lab_send.at[i], lab_recv.at[z], {"dp": o})
+        remote(lab.at[z], lab.at[z], lab_send.at[i], lab_recv.at[z], {"dp": o})
         for i, o in enumerate(others(z))
     ]
     for copy in lab_copies:
         copy.start()
+
+    train_in.wait()
 
     @pl.loop(0, CHUNKS)
     def _(c):
@@ -213,12 +224,14 @@
     end = pl.ds(local, BLK)
 
     he_left = remote(
-        held.at[:, pl.ds(0, BLK)], hext.at[:, last], he_send.at[0], he_recv.at[1], left
+        hext.at[:, head], hext.at[:, last], he_send.at[0], he_recv.at[1], left
     )
     he_right = remote(
-        held.at[:, pl.ds(local - BLK, BLK)], hext.at[:, first], he_send.at[1], he_recv.at[0], right
+        hext.at[:, end], hext.at[:, first], he_send.at[1], he_recv.at[0], right
     )
 
+    held_in.wait()
+
     @pl.when(f > 0)
     def _():
         he_left.start()
@@ -228,8 +241,6 @@
         he_right.start()
 
     tf[z] = train[...]
-    lab[z] = labels[...]
-    hext[:, pl.ds(BLK, local)] = held[...]
 
     @pl.when(f == 0)
     def _():
@@ -257,6 +268,17 @@
 
     def block(i):
         return pl.ds(pl.multiple_of(i * BLK, BLK), BLK)
+
+    for i, o in enumerate(others(z)):
+        remote(lab.at[o], lab.at[o], lab_send.at[i], lab_recv.at[o], {"dp": o}).wait_recv()
+    counts = jnp.zeros((C, 1), F32)
+    for o in range(n):
+        ids = lax.broadcasted_iota(jnp.int32, (C, rows), 0)
+        hot = (lab[o, 0:1, :] == ids).astype(F32)
+        onehot_t[o] = hot.astype(BF16)
+        counts += jnp.sum(hot, axis=1, keepdims=True)
+    inverse = 1.0 / counts
+    prec_in.wait()
 
     @pl.loop(0, nloc)
     def _(m):
@@ -265,30 +287,29 @@
             total += nt(hext[:, block(m + k)], prec[k, block(m), :])
         img[:, block(m)] = total
 
-    for i, o in enumerate(others(z)):
-        remote(labels, lab.at[o], lab_send.at[i], lab_recv.at[o], {"dp": o}).wait_recv()
-    for o in range(n):
-        ids = lax.broadcasted_iota(jnp.int32, (C, rows), 0)
-        onehot_t[:, o * rows : (o + 1) * rows] = (lab[o, 0:1, :] == ids).astype(F32).astype(BF16)
-
-    def out_copies(o):
-        where = pl.ds(pl.multiple_of(o * rows, rows), rows)
-        return (
-            pltpu.make_async_copy(tf.at[o], lhs.at[where], out_sem.at[0, o]),
-            pltpu.make_async_copy(td.at[o], rhs.at[where], out_sem.at[1, o]),
-        )
-
     @pl.loop(0, CHUNKS)
     def _(c):
         td_event(z, c)
 
+    def absorb_f(o, m):
+        sf[:, block(m)] += nn(onehot_t[o], tf[o, :, block(m)])
+
+    def absorb_d(o, m):
+        sd[:, block(m)] += nn(onehot_t[o], td[o, :, block(m)])
+        cov[block(m), :] += contract_rows(tf[o, :, block(m)], td[o])
+
+    def first_piece(m):
+        sf[:, block(m)] = nn(onehot_t[z], tf[z, :, block(m)])
+        sd[:, block(m)] = nn(onehot_t[z], td[z, :, block(m)])
+        cov[block(m), :] = contract_rows(tf[z, :, block(m)], td[z])
+
     for s in range(1, n):
 
-        @pl.loop(0, CHUNKS + 1)
+        @pl.loop(0, CHUNKS)
         def _(c, s=s):
             for o in (z - s, z + s):
 
-                @pl.when((o >= 0) & (o < n) & (c < CHUNKS))
+                @pl.when((o >= 0) & (o < n))
                 def _():
                     tf_event(o, c)
 
@@ -298,18 +319,34 @@
                 def _():
                     td_event(o, c - 1)
 
-    for o in range(n):
-        for copy in out_copies(o):
-            copy.start()
-
-    counts = jnp.sum(onehot_t[...].astype(F32), axis=1, keepdims=True)
-    inverse = 1.0 / counts
+            if s == 1:
+                first_piece(c)
+            else:
+                for o in (z - s + 1, z + s - 1):
+
+                    @pl.when((o >= 0) & (o < n))
+                    def _():
+                        absorb_f(o, c)
+                        absorb_d(o, c)
+
+        if s < n - 1:
+            for o in (z - s, z + s):
+
+                @pl.when((o >= 0) & (o < n))
+                def _():
+                    td_event(o, CHUNKS - 1)
+
+    for o in (z - n + 1, z + n - 1):
+
+        @pl.when((o >= 0) & (o < n))
+        def _():
+            @pl.loop(0, nloc)
+            def _(m):
+                absorb_f(o, m)
 
     @pl.loop(0, nloc)
     def _(m):
-        total = nn(onehot_t[:, 0:rows], tf[0, :, block(m)])
-        for o in range(1, n):
-            total += nn(onehot_t[:, o * rows : (o + 1) * rows], tf[o, :, block(m)])
+        total = sf[:, block(m)]
         high, low = split(total)
         tail_l[0:C, block(m)] = high
         tail_l[C : 2 * C, block(m)] = high
@@ -337,23 +374,32 @@
         for copy in me_right:
             copy.start()
 
+    for o in (z - n + 1, z + n - 1):
+
+        @pl.when((o >= 0) & (o < n))
+        def _():
+            td_event(o, CHUNKS - 1)
+
+            @pl.loop(0, nloc)
+            def _(m):
+                absorb_d(o, m)
+
     @pl.loop(0, nloc)
     def _(m):
-        total = nn(onehot_t[:, 0:rows], td[0, :, block(m)])
-        for o in range(1, n):
-            total += nn(onehot_t[:, o * rows : (o + 1) * rows], td[o, :, block(m)])
-        high, low = split(-(total * inverse))
+        high, low = split(-(sd[:, block(m)] * inverse))
         tail_r[0:C, block(m)] = high
         tail_r[C : 2 * C, block(m)] = low
         tail_r[2 * C : 3 * C, block(m)] = high
 
-    below = pl.ds(n * rows, 3 * C)
-    tail_copies = (
-        pltpu.make_async_copy(tail_l, lhs.at[below], out_sem.at[0, n]),
-        pltpu.make_async_copy(tail_r, rhs.at[below], out_sem.at[1, n]),
-    )
-    for copy in tail_copies:
-        copy.start()
+    scale = 1.0 / float(rows * n - C)
+
+    def finish(m):
+        total = cov[block(m), :] + contract_rows(tail_l[:, block(m)], tail_r[...])
+        cov[block(m), :] = total * scale
+
+    @pl.loop(0, nloc // 2)
+    def _(m):
+        finish(m)
 
     @pl.when(f > 0)
     def _():
@@ -378,7 +424,7 @@
         image = img[:, block(m)] - (nn(pick, high) + nn(pick, low))
         white[:, block(m)] = image.astype(BF16)
         picked = nn(pick, mhi[:, block(m + 1)]) + nn(pick, mlo[:, block(m + 1)])
-        score = (held[:, block(m)].astype(F32) - picked) * image
+        score = (hext[:, block(m + 1)].astype(F32) - picked) * image
         dacc[...] += score[:, 0:128] + score[:, 128:256]
 
     row = jnp.sum(dacc[...].T, axis=0, keepdims=True)
@@ -389,6 +435,11 @@
     ]
     for copy in ds_copies:
         copy.start()
+
+    @pl.loop(nloc // 2, nloc)
+    def _(m):
+        finish(m)
+
     for i, o in enumerate(others(f)):
         remote(dsend, drecv.at[o], ds_send.at[i], ds_recv.at[o], {"feat": o}).wait_recv()
     total = row
@@ -431,36 +482,32 @@
         def _():
             sib_copy(o, c, src).wait_send()
 
-    for o in range(n):
-        for copy in out_copies(o):
-            copy.wait()
-    for copy in tail_copies:
-        copy.wait()
-
 
 def square_body(train_rows, train_labels, held_rows, held_labels, precision):
     rows, local = train_rows.shape
     nheld = held_rows.shape[0]
     n = lax.axis_size("dp")
-    labels = jnp.broadcast_to(train_labels.reshape(1, rows), (8, rows))
-    hlabels = jnp.broadcast_to(held_labels.reshape(1, nheld), (8, nheld))
-    depth = n * rows + 3 * C
+    labels = train_labels.reshape(1, rows)
+    hlabels = held_labels.reshape(1, nheld)
     vmem = pl.BlockSpec(memory_space=pltpu.VMEM)
-    hbm = pl.BlockSpec(memory_space=pl.ANY)
+    hbm = pl.BlockSpec(memory_space=pltpu.HBM)
     dma = pltpu.SemaphoreType.DMA
-    lhs, rhs, white, dist = pl.pallas_call(
+    cov, white, dist = pl.pallas_call(
         gather_kernel,
         out_shape=(
-            jax.ShapeDtypeStruct((depth, local), BF16),
-            jax.ShapeDtypeStruct((depth, local), BF16),
+            jax.ShapeDtypeStruct((local, local), F32),
             jax.ShapeDtypeStruct((nheld, local), BF16),
             jax.ShapeDtypeStruct((1, nheld), F32),
         ),
-        in_specs=[vmem] * 5,
-        out_specs=(hbm, hbm, vmem, vmem),
+        in_specs=[hbm, vmem, hbm, vmem, hbm],
+        out_specs=(vmem, vmem, vmem),
         scratch_shapes=[
+            pltpu.VMEM((rows, local), BF16),
+            pltpu.VMEM(precision.shape, BF16),
             pltpu.VMEM((n, rows, local), BF16),
             pltpu.VMEM((n, rows, local), BF16),
+            pltpu.VMEM((C, local), F32),
+            pltpu.VMEM((C, local), F32),
             pltpu.VMEM((3 * C, local), BF16),
             pltpu.VMEM((3 * C, local), BF16),
             pltpu.VMEM((n, 8, rows), jnp.int32),
@@ -468,7 +515,7 @@
             pltpu.VMEM((C, local + 2 * BLK), BF16),
             pltpu.VMEM((C, local + 2 * BLK), BF16),
             pltpu.VMEM((nheld, local), F32),
-            pltpu.VMEM((C, n * rows), BF16),
+            pltpu.VMEM((n, C, rows), BF16),
             pltpu.VMEM((nheld, C), BF16),
             pltpu.VMEM((nheld, 128), F32),
             pltpu.VMEM((8, nheld), F32),
@@ -488,14 +535,13 @@
             dma((n - 1,)),
             dma((n,)),
             dma((n, CHUNKS)),
-            dma((2, n + 1)),
+            dma((3,)),
         ],
         compiler_params=pltpu.CompilerParams(
             collective_id=0, has_side_effects=True, vmem_limit_bytes=40 * 1024 * 1024
         ),
     )(train_rows, labels, held_rows, hlabels, precision)
-    pooled_cov = contract_rows(lhs, rhs) * (1.0 / float(rows * n - C))
-    return pooled_cov, white, dist.reshape(nheld)
+    return cov, white, dist.reshape(nheld)
 
 
 def solution(mesh):

time: 73.7 us -> 70.6 us (0.958)
  matrix products: 5.55 us -> 0 us
  local copies, waits for them, and re-layouts: 6.58 us -> 8.59 us
    dot_general x1 -> x0, matrix products: 5.55 us -> none  [contract_rows(): lax.dot_general(left, right, (((0,), (0,)), ((), ())), preferred_element_...]
    unnamed x8 -> x13, local copies, waits for them, and re-layouts: 5.22 us -> 8.59 us
    broadcast_in_dim x2 -> x0, local copies, waits for them, and re-layouts: 1.36 us -> none  [the longest x1 0.68 us: square_body(): hlabels = jnp.broadcast_to(held_labels.reshape(1, nheld), (8, nheld))]
where the time goes in v2:
time: 70.6 us; the launch traced here: 70.3 us
  Pallas kernels  61.1 us (87%)
  local copies, waits for them, and re-layouts  8.59 us (12%)
    pallas_call x1, Pallas kernels, square_body(): pl.pallas_call(gather_kernel, out_shape=(jax.ShapeDtypeStruct((local, loc...  61.1 us
    unnamed x13, local copies, waits for them, and re-layouts  8.59 us

profile of v2, /device:TPU:0, one launch (start us, length us, event | category | flops | bytes accessed | tf_op | source)
XLA Modules:
  0.0 70.3 jit_solution(11888145525948663885)
XLA Ops:
  0.6 0.0 copy-start
  0.6 1.4 %copy-done = bf16[3,1024,256]{2,1,0:T(8,128)(2,1)S(1)} copy-done((bf16[3,1024,256]{2,1,0:T(8,128)(2,1)S(1)}, bf16[3,1024,256]{2,1,0:T(8,128)(2,1)}, u32[]{:S(2)}) %copy-start) | copy-done | bytes 1572888
  2.0 0.0 copy-start.1
  2.0 1.2 %copy-done.1 = bf16[512,1024]{1,0:T(8,128)(2,1)S(1)} copy-done((bf16[512,1024]{1,0:T(8,128)(2,1)S(1)}, bf16[512,1024]{1,0:T(8,128)(2,1)}, u32[]{:S(2)}) %copy-start.1) | copy-done | bytes 1048600
  3.3 0.0 copy-start.2
  3.3 1.0 %copy-done.2 = bf16[256,1024]{1,0:T(8,128)(2,1)S(1)} copy-done((bf16[256,1024]{1,0:T(8,128)(2,1)S(1)}, bf16[256,1024]{1,0:T(8,128)(2,1)}, u32[]{:S(2)}) %copy-start.2) | copy-done | bytes 524312
  4.3 0.0 copy-start.3
  4.3 0.7 copy-done.3
  5.0 0.0 copy-start.4
  5.0 0.7 copy-done.4
  5.7 61.1 %shard_map.76 = (f32[1024,1024]{1,0:T(8,128)S(1)}, bf16[512,1024]{1,0:T(8,128)(2,1)S(1)}, f32[1,512]{1,0:T(1,128)S(1)}) custom-call(bf16[256,1024]{1,0:T(8,128)(2,1)S(1)} %copy-done.2, s32[1,256]{1,0:T(1,128)S(1)} %bitcast.5, bf16[512,1024]{1,0:T(8,128)(2,1)S(1)} %copy-done.1, s32[1,512]{1,0:T(1,128)S(1)} %bitcast.3, bf16[3,1024,256]{2,1,0:T(8,128)(2,1)S(1)} %copy-done), custom_call_target="tpu_custom_call" | custom-call | tf_op jit(solution)/shard_map/pallas_call | solution.py:495
  66.8 2.0 %copy.11 = f32[1024,1024]{1,0:T(8,128)} copy(f32[1024,1024]{1,0:T(8,128)S(1)} %get-tuple-element.12) | data formatting | bytes 8388608
  68.8 1.0 %copy.12 = bf16[512,1024]{1,0:T(8,128)(2,1)} copy(bf16[512,1024]{1,0:T(8,128)(2,1)S(1)} %get-tuple-element.13) | data formatting | bytes 2097152
  69.8 0.6 copy.13
Async XLA Ops:
  0.6 1.4 %copy-start = (bf16[3,1024,256]{2,1,0:T(8,128)(2,1)S(1)}, bf16[3,1024,256]{2,1,0:T(8,128)(2,1)}, u32[]{:S(2)}) copy-start(bf16[3,1024,256]{2,1,0:T(8,128)(2,1)} %prec_hbm.1) | copy-start | bytes 4718596
  2.0 1.2 %copy-start.1 = (bf16[512,1024]{1,0:T(8,128)(2,1)S(1)}, bf16[512,1024]{1,0:T(8,128)(2,1)}, u32[]{:S(2)}) copy-start(bf16[512,1024]{1,0:T(8,128)(2,1)} %held_hbm.1) | copy-start | bytes 3145732
  3.3 1.0 %copy-start.2 = (bf16[256,1024]{1,0:T(8,128)(2,1)S(1)}, bf16[256,1024]{1,0:T(8,128)(2,1)}, u32[]{:S(2)}) copy-start(bf16[256,1024]{1,0:T(8,128)(2,1)} %train_hbm.1) | copy-start | bytes 1572868
  4.3 0.7 copy-start.3
  5.0 0.7 copy-start.4

commit v3 on v2

--- a/solution.py
+++ b/solution.py
@@ -121,6 +121,7 @@
     ochip = 1 - chip
     root = f == z
     near = chip == z // 2
+    at_end = (z == 0) | (z == n - 1)
 
     def others(i):
         return [lax.rem(i + s, n) for s in range(1, n)]
@@ -177,8 +178,8 @@
 
         @pl.when(root)
         def _():
+            sib_copy(o, c, src).start()
             och_copy(o, c, src).start()
-            sib_copy(o, c, src).start()
             own_copy(o, c, src).start()
 
     def tf_event(o, c):
@@ -321,10 +322,15 @@
 
             if s == 1:
                 first_piece(c)
-            else:
-                for o in (z - s + 1, z + s - 1):
-
-                    @pl.when((o >= 0) & (o < n))
+            for t in range(1, s):
+                for o in (z - t, z + t):
+                    ready = (o >= 0) & (o < n)
+                    if s < n - 1:
+                        ready = ready & at_end & (t == s - 1)
+                    elif t < s - 1:
+                        ready = ready & jnp.logical_not(at_end)
+
+                    @pl.when(ready)
                     def _():
                         absorb_f(o, c)
                         absorb_d(o, c)
@@ -383,23 +389,6 @@
             @pl.loop(0, nloc)
             def _(m):
                 absorb_d(o, m)
-
-    @pl.loop(0, nloc)
-    def _(m):
-        high, low = split(-(sd[:, block(m)] * inverse))
-        tail_r[0:C, block(m)] = high
-        tail_r[C : 2 * C, block(m)] = low
-        tail_r[2 * C : 3 * C, block(m)] = high
-
-    scale = 1.0 / float(rows * n - C)
-
-    def finish(m):
-        total = cov[block(m), :] + contract_rows(tail_l[:, block(m)], tail_r[...])
-        cov[block(m), :] = total * scale
-
-    @pl.loop(0, nloc // 2)
-    def _(m):
-        finish(m)
 
     @pl.when(f > 0)
     def _():
@@ -436,9 +425,19 @@
     for copy in ds_copies:
         copy.start()
 
-    @pl.loop(nloc // 2, nloc)
+    @pl.loop(0, nloc)
     def _(m):
-        finish(m)
+        high, low = split(-(sd[:, block(m)] * inverse))
+        tail_r[0:C, block(m)] = high
+        tail_r[C : 2 * C, block(m)] = low
+        tail_r[2 * C : 3 * C, block(m)] = high
+
+    scale = 1.0 / float(rows * n - C)
+
+    @pl.loop(0, nloc)
+    def _(m):
+        total = cov[block(m), :] + contract_rows(tail_l[:, block(m)], tail_r[...])
+        cov[block(m), :] = total * scale
 
     for i, o in enumerate(others(f)):
         remote(dsend, drecv.at[o], ds_send.at[i], ds_recv.at[o], {"feat": o}).wait_recv()

time: 70.6 us -> 69.9 us (0.990); the launches traced: 70.3 us -> 68.8 us
  Pallas kernels: 61.1 us -> 59.5 us
    pallas_call x1, Pallas kernels: 61.1 us -> 59.5 us  [square_body(): pl.pallas_call(gather_kernel, out_shape=(jax.ShapeDtypeStruct((local, loc...]
where the time goes in v3:
time: 69.9 us; the launch traced here: 68.8 us
  Pallas kernels  59.5 us (85%)
  local copies, waits for them, and re-layouts  8.59 us (12%)
    pallas_call x1, Pallas kernels, square_body(): pl.pallas_call(gather_kernel, out_shape=(jax.ShapeDtypeStruct((local, loc...  59.5 us
    unnamed x13, local copies, waits for them, and re-layouts  8.59 us

profile of v3, /device:TPU:0, one launch (start us, length us, event | category | flops | bytes accessed | tf_op | source)
XLA Modules:
  0.0 68.8 jit_solution(9866546941887447804)
XLA Ops:
  0.6 0.0 copy-start
  0.6 1.4 %copy-done = bf16[3,1024,256]{2,1,0:T(8,128)(2,1)S(1)} copy-done((bf16[3,1024,256]{2,1,0:T(8,128)(2,1)S(1)}, bf16[3,1024,256]{2,1,0:T(8,128)(2,1)}, u32[]{:S(2)}) %copy-start) | copy-done | bytes 1572888
  2.0 0.0 copy-start.1
  2.0 1.2 %copy-done.1 = bf16[512,1024]{1,0:T(8,128)(2,1)S(1)} copy-done((bf16[512,1024]{1,0:T(8,128)(2,1)S(1)}, bf16[512,1024]{1,0:T(8,128)(2,1)}, u32[]{:S(2)}) %copy-start.1) | copy-done | bytes 1048600
  3.3 0.0 copy-start.2
  3.3 1.0 %copy-done.2 = bf16[256,1024]{1,0:T(8,128)(2,1)S(1)} copy-done((bf16[256,1024]{1,0:T(8,128)(2,1)S(1)}, bf16[256,1024]{1,0:T(8,128)(2,1)}, u32[]{:S(2)}) %copy-start.2) | copy-done | bytes 524312
  4.3 0.0 copy-start.3
  4.3 0.7 copy-done.3
  5.0 0.0 copy-start.4
  5.0 0.7 copy-done.4
  5.7 59.5 %shard_map.76 = (f32[1024,1024]{1,0:T(8,128)S(1)}, bf16[512,1024]{1,0:T(8,128)(2,1)S(1)}, f32[1,512]{1,0:T(1,128)S(1)}) custom-call(bf16[256,1024]{1,0:T(8,128)(2,1)S(1)} %copy-done.2, s32[1,256]{1,0:T(1,128)S(1)} %bitcast.5, bf16[512,1024]{1,0:T(8,128)(2,1)S(1)} %copy-done.1, s32[1,512]{1,0:T(1,128)S(1)} %bitcast.3, bf16[3,1024,256]{2,1,0:T(8,128)(2,1)S(1)} %copy-done), custom_call_target="tpu_custom_call" | custom-call | tf_op jit(solution)/shard_map/pallas_call | solution.py:494
  65.2 2.0 %copy.11 = f32[1024,1024]{1,0:T(8,128)} copy(f32[1024,1024]{1,0:T(8,128)S(1)} %get-tuple-element.12) | data formatting | bytes 8388608
  67.2 1.0 %copy.12 = bf16[512,1024]{1,0:T(8,128)(2,1)} copy(bf16[512,1024]{1,0:T(8,128)(2,1)S(1)} %get-tuple-element.13) | data formatting | bytes 2097152
  68.2 0.6 copy.13
Async XLA Ops:
  0.6 1.4 %copy-start = (bf16[3,1024,256]{2,1,0:T(8,128)(2,1)S(1)}, bf16[3,1024,256]{2,1,0:T(8,128)(2,1)}, u32[]{:S(2)}) copy-start(bf16[3,1024,256]{2,1,0:T(8,128)(2,1)} %prec_hbm.1) | copy-start | bytes 4718596
  2.0 1.2 %copy-start.1 = (bf16[512,1024]{1,0:T(8,128)(2,1)S(1)}, bf16[512,1024]{1,0:T(8,128)(2,1)}, u32[]{:S(2)}) copy-start(bf16[512,1024]{1,0:T(8,128)(2,1)} %held_hbm.1) | copy-start | bytes 3145732
  3.3 1.0 %copy-start.2 = (bf16[256,1024]{1,0:T(8,128)(2,1)S(1)}, bf16[256,1024]{1,0:T(8,128)(2,1)}, u32[]{:S(2)}) copy-start(bf16[256,1024]{1,0:T(8,128)(2,1)} %train_hbm.1) | copy-start | bytes 1572868
  4.3 0.7 copy-start.3
  5.0 0.7 copy-start.4
